TPU v7x, 256 devices: a whole 4x4x8 slice. The times are simulated.
256 devices in a mesh: group: 32 (over y, z), local: 8 (over x, core).
Axes of the slice: x: 4, y: 4, z: 8, core: 2. Of those that a mesh axis runs over, the one named last changes fastest.
Arguments:
- tokens: bfloat16 [2048, 7168], P('group', 'local'), may hold values from -6 to 6
- routes: int32 [2048, 8], P('group'), may hold values from 0 to 31, as said below
- affinity: float32 [2048, 8], P('group'), may hold values from 0.05 to 0.6
- gate_proj: bfloat16 [32, 7168, 2048], P('group', None, 'local'), may hold values from -0.0625 to 0.0625
- up_proj: bfloat16 [32, 7168, 2048], P('group', None, 'local'), may hold values from -0.0625 to 0.0625
- down_proj: bfloat16 [32, 2048, 7168], P('group', None, 'local'), may hold values from -0.125 to 0.125
Outputs:
- combined: bfloat16 [2048, 7168], P('group', 'local')
Inputs may be any that keep to these rules, and one draw needn't show every extreme that they name: `routes`: each token names 8 distinct experts, two in each of 4 node groups (node group n holds experts n * 4 to (n + 1) * 4 - 1); in each block of 64 tokens every node group is named by exactly half of the tokens, no expert is named by more than 24 tokens, and one expert of every node group, the same in all blocks, is named by exactly 24 tokens of every block.
All inputs are finite; a program needn't handle non-finite values.
Results may differ from a plain program's by a relative error of at most 0.0058.
Values may be sent and summed in bfloat16 or wider, within the bound.
A program may use at most 64 MiB of HBM per device.

v0:
```python
import jax
import jax.numpy as jnp
from jax import lax
from jax.sharding import PartitionSpec as P


def block_slots(routes_block, experts):
    chosen = (
        routes_block[:, :, None] == jnp.arange(experts, dtype=jnp.int32)[None, None, :]
    ).astype(jnp.int32)
    per_token = jnp.sum(chosen, axis=1)
    earlier = jnp.cumsum(per_token, axis=0) - per_token
    return jnp.sum(chosen * earlier[:, None, :], axis=2)


def slot_owner(routes_block, slot_index, capacity, experts):
    flat_slot = (routes_block * capacity + slot_index).reshape(-1)
    token_ids = jnp.broadcast_to(
        jnp.arange(routes_block.shape[0], dtype=jnp.int32)[:, None], routes_block.shape
    ).reshape(-1)
    owner_table = jnp.full((experts * capacity,), -1, dtype=jnp.int32)
    return owner_table.at[flat_slot].set(token_ids)


def on_device(tokens, routes, affinity, gate_proj, up_proj, down_proj):
    groups = lax.axis_size("group")
    experts = max(groups, 16)
    per_group = experts // groups
    tok_count = tokens.shape[0]
    top_count = routes.shape[1]
    capacity = min(3 * tok_count * top_count // (2 * experts), tok_count // 2)
    slot_index = block_slots(routes, experts)
    owners = slot_owner(routes, slot_index, capacity, experts)
    present = (owners >= 0)[:, None]
    safe_owner = jnp.maximum(owners, 0)
    outgoing = jnp.where(present, tokens[safe_owner], jnp.zeros((), jnp.bfloat16))
    outgoing = outgoing.reshape(groups, per_group, capacity, tokens.shape[1])
    portion = lax.all_gather(
        lax.all_to_all(outgoing, "group", split_axis=0, concat_axis=0, tiled=True),
        "local",
        axis=3,
        tiled=True,
    )
    gate_more = jnp.einsum("sjcd,jdh->sjch", portion, gate_proj, preferred_element_type=jnp.float32)
    up_more = jnp.einsum("sjcd,jdh->sjch", portion, up_proj, preferred_element_type=jnp.float32)
    hidden_part = (jax.nn.silu(gate_more) * up_more).astype(jnp.bfloat16)
    outputs = jnp.einsum(
        "sjch,jhf->sjcf",
        lax.all_gather(hidden_part, "local", axis=3, tiled=True),
        down_proj,
        preferred_element_type=jnp.float32,
    )
    returned = lax.all_to_all(
        outputs.astype(jnp.bfloat16), "group", split_axis=0, concat_axis=0, tiled=True
    )
    flat_rows = returned.reshape(experts * capacity, returned.shape[3])
    flat_index = routes * capacity + slot_index
    picked = flat_rows[flat_index]
    combined = jnp.sum(picked.astype(jnp.float32) * affinity[:, :, None], axis=1)
    return combined.astype(jnp.bfloat16)


def solution(mesh):
    in_specs = (
        P("group", "local"),
        P("group", None),
        P("group", None),
        P("group", None, "local"),
        P("group", None, "local"),
        P("group", None, "local"),
    )
    out_specs = P("group", "local")
    return jax.shard_map(
        on_device, mesh=mesh, in_specs=in_specs, out_specs=out_specs, check_vma=False
    )
```

profile of v0, /device:TPU:97, one launch (start us, length us, event | category | flops | bytes accessed | tf_op | source)
XLA Modules:
  0.0 229.8 jit_solution(9742206043245930512)
XLA Ops:
  6.5 0.7 convert_reduce_fusion
  7.3 0.1 copy.20
  7.4 0.1 reduce_window_sum.11
  7.5 0.1 copy.22
  7.5 0.7 select_reduce_fusion
  8.3 0.7 compare_select_fusion.1
  9.0 0.1 copy.23
  9.1 0.1 reshape.87
  9.2 0.1 reshape.115
  9.3 2.4 %scatter_custom_fusion = s32[768]{0:T(1024)S(1)} fusion(s32[512]{0:T(512)S(1)} %bitcast.80, s32[512]{0:T(512)S(1)} %reshape.115, s32[]{:T(128)} %constant.7.clone.1), kind=kCustom, calls=%fused_computation.31 | custom fusion | bytes 3076 | tf_op jit(solution)/shard_map/scatter | solution.py:22
  11.8 0.1 broadcast_in_dim.37
  11.9 2.8 %gather_fusion = bf16[768,896]{1,0:T(8,128)(2,1)S(1)} fusion(bf16[64,896]{1,0:T(8,128)(2,1)S(1)} %copy-done, s32[1024]{0:T(1024)S(1)} %pad_clamp_fusion.1), kind=kCustom, calls=%fused_computation | custom fusion | bytes 2755584 | tf_op jit(solution)/shard_map/gather | solution.py:36
  14.7 0.2 broadcast_select_fusion
  14.9 42.3 %all_to_all.10 = bf16[32,1,24,896]{3,2,1,0:T(8,128)(2,1)} all-to-all(bf16[32,1,24,896]{3,2,1,0:T(8,128)(2,1)S(1)} %broadcast_select_fusion), channel_id=1, replica_groups=mesh['group'=32,'local'=8] {'group'}, dimensions={0} | all-to-all | bytes 2752512 | tf_op jit(solution)/shard_map/all_to_all | solution.py:39
  57.2 0.0 all-gather.3.cloned.1.call-update
  57.3 0.0 all-gather.5.cloned.1.call-start
  57.3 63.9 %all-gather.3.cloned.1.call-done = bf16[32,1,24,7168]{3,2,0,1:T(8,128)(2,1)} async-done(((bf16[32,1,24,896]{3,2,0,1:T(8,128)(2,1)}), bf16[32,1,24,7168]{3,2,0,1:T(8,128)(2,1)}) %all-gather.3.cloned.1.call-update) | async-done | bytes 11010064 | tf_op jit(solution)/shard_map/all_gather | solution.py:38
  121.2 7.0 %fusion.20 = f32[32,1,24,256]{3,2,0,1:T(8,128)S(1)} fusion(bf16[1,7168,256]{2,1,0:T(8,128)(2,1)} %param.9, bf16[32,1,24,7168]{3,2,0,1:T(8,128)(2,1)} %all-gather.3.cloned.1.call-done), kind=kOutput, calls=%fused_computation.17 | convolution fusion | flops 2818572288 | bytes 15466496 | tf_op jit(solution)/shard_map/sjcd,jdh->sjch/dot_general | solution.py:44
  128.2 1.3 copy-done.2
  129.6 1.0 copy-done.3
  130.6 3.8 %fusion.35 = bf16[32,1,24,256]{3,2,0,1:T(8,128)(2,1)} fusion(bf16[1,7168,256]{2,1,0:T(8,128)(2,1)S(1)} %copy-done.3, bf16[32,1,24,7168]{3,2,0,1:T(8,128)(2,1)S(1)} %copy-done.2, f32[32,1,24,256]{3,2,0,1:T(8,128)S(1)} %fusion.20), kind=kOutput, calls=%fused_computation.20 | convolution fusion | flops 2819751936 | bytes 15859712 | tf_op jit(solution)/shard_map/sjcd,jdh->sjch/dot_general | solution.py:45
  134.3 0.0 all-gather.5.cloned.1.call-update
  134.4 0.0 copy-start.1
  134.4 34.7 %all-gather.5.cloned.1.call-done = bf16[32,1,24,2048]{3,2,0,1:T(8,128)(2,1)} async-done(((bf16[32,1,24,256]{3,2,0,1:T(8,128)(2,1)}), bf16[32,1,24,2048]{3,2,0,1:T(8,128)(2,1)}) %all-gather.5.cloned.1.call-update) | async-done | bytes 3145744 | tf_op jit(solution)/shard_map/all_gather | solution.py:49
  169.1 7.5 %fusion.15 = bf16[32,1,24,896]{3,2,1,0:T(8,128)(2,1)} fusion(bf16[1,2048,896]{2,1,0:T(8,128)(2,1)} %param.11, bf16[32,1,24,2048]{3,2,0,1:T(8,128)(2,1)} %all-gather.5.cloned.1.call-done), kind=kOutput, calls=%fused_computation.15 | convolution fusion | flops 2819260416 | bytes 8192000 | tf_op jit(solution)/shard_map/sjch,jhf->sjcf/dot_general | solution.py:47
  176.6 9.3 %all-to-all-start.1 = ((bf16[32,1,24,896]{3,2,1,0:T(8,128)(2,1)}), bf16[32,1,24,896]{3,2,1,0:T(8,128)(2,1)S(1)}, u32[]{:S(2)}, u32[]{:S(2)}) async-start(bf16[32,1,24,896]{3,2,1,0:T(8,128)(2,1)} %fusion.15), calls=%async_computation.1 | async-start | bytes 2752512 | tf_op jit(solution)/shard_map/all_to_all | solution.py:53
  186.0 0.1 copy.27
  186.1 0.1 reshape.105
  186.2 0.1 copy.28
  186.3 33.4 %all-to-all-done.1 = bf16[32,1,24,896]{3,2,1,0:T(8,128)(2,1)S(1)} async-done(((bf16[32,1,24,896]{3,2,1,0:T(8,128)(2,1)}), bf16[32,1,24,896]{3,2,1,0:T(8,128)(2,1)S(1)}, u32[]{:S(2)}, u32[]{:S(2)}) %all-to-all-start.1) | async-done | bytes 1376288 | tf_op jit(solution)/shard_map/all_to_all | solution.py:53
  219.7 2.0 gather_fusion.1
  221.7 1.3 fusion.9
  (13 shorter events, 0.1 us)
Async XLA Ops:
  6.5 5.3 %copy-start = (bf16[64,896]{1,0:T(8,128)(2,1)S(1)}, bf16[64,896]{1,0:T(8,128)(2,1)}, u32[]{:S(2)}) copy-start(bf16[64,896]{1,0:T(8,128)(2,1)} %param.6) | copy-start | bytes 344068
  6.5 114.7 %all-gather.3.cloned.1.call-start = ((), (), s32[]{:S(2)}) async-start(), calls=%async_computation.2 | async-start | bytes 12386304 | tf_op jit(solution)/shard_map/all_gather | solution.py:38
  57.3 111.9 %all-gather.5.cloned.1.call-start = ((), (), s32[]{:S(2)}) async-start(), calls=%async_computation.3 | async-start | bytes 3538944 | tf_op jit(solution)/shard_map/all_gather | solution.py:49
  121.2 8.4 %copy-start.2 = (bf16[32,1,24,7168]{3,2,0,1:T(8,128)(2,1)S(1)}, bf16[32,1,24,7168]{3,2,0,1:T(8,128)(2,1)}, u32[]{:S(2)}) copy-start(bf16[32,1,24,7168]{3,2,0,1:T(8,128)(2,1)} %all-gather.3.cloned.1.call-done) | copy-start | bytes 33030148
  121.2 9.4 %copy-start.3 = (bf16[1,7168,256]{2,1,0:T(8,128)(2,1)S(1)}, bf16[1,7168,256]{2,1,0:T(8,128)(2,1)}, u32[]{:S(2)}) copy-start(bf16[1,7168,256]{2,1,0:T(8,128)(2,1)} %param.10) | copy-start | bytes 11010052
  134.4 51.8 %copy-start.1 = (f32[64,8]{0,1:T(8,128)S(1)}, f32[64,8]{0,1:T(8,128)}, u32[]{:S(2)}) copy-start(f32[64,8]{0,1:T(8,128)} %param.8) | copy-start | bytes 6148
  176.6 43.0 %all-to-all-start.1 = ((bf16[32,1,24,896]{3,2,1,0:T(8,128)(2,1)}), bf16[32,1,24,896]{3,2,1,0:T(8,128)(2,1)S(1)}, u32[]{:S(2)}, u32[]{:S(2)}) async-start(bf16[32,1,24,896]{3,2,1,0:T(8,128)(2,1)} %fusion.15), calls=%async_computation.1 | async-start | bytes 2752512 | tf_op jit(solution)/shard_map/all_to_all | solution.py:53
Sparse Core Ops, SparseCore 0:
  57.4 63.7 all-gather.2
  134.5 34.5 all-gather.4
where the time goes:
time: 233 us; the launch traced here: 230 us
  waiting for transfers between devices  132 us (57%)
  blocking collectives  42.3 us (18%)
  matrix products  18.3 us (8%)
  between operations  13.5 us (6%)
  local copies, waits for them, and re-layouts  10.4 us (4%)
  starting transfers between devices  9.39 us (4%)
  other arithmetic  3.8 us (2%)
    all_gather x1, waiting for transfers between devices, on_device(): lax.all_gather(lax.all_to_all(outgoing, 'group', split_axis=0, concat_axi...  63.9 us
    all_to_all x1, blocking collectives, on_device(): lax.all_to_all(outgoing, 'group', split_axis=0, concat_axis=0, tiled=True)  42.3 us
    all_gather x1, waiting for transfers between devices, on_device(): lax.all_gather(hidden_part, 'local', axis=3, tiled=True)  34.7 us
    all_to_all x1, waiting for transfers between devices, on_device(): lax.all_to_all(outputs.astype(jnp.bfloat16), 'group', split_axis=0, conca...  33.4 us
    all_to_all x1, starting transfers between devices, on_device(): lax.all_to_all(outputs.astype(jnp.bfloat16), 'group', split_axis=0, conca...  9.34 us
    dot_general x1, matrix products, on_device(): jnp.einsum('sjch,jhf->sjcf', lax.all_gather(hidden_part, 'local', axis=3,...  7.51 us
    dot_general x1, matrix products, on_device(): jnp.einsum('sjcd,jdh->sjch', portion, gate_proj, preferred_element_type=j...  7.04 us
  transfers between devices with their start and end apart: 3, of which 3 were waited for; matrix products, arithmetic and copies ran while one was open for 0% of the time, Pallas kernels for 0%

commit v1 on v0

v1 whole, which is shorter than its diff:
```python
import jax
import jax.numpy as jnp
from jax import lax
from jax.experimental import pallas as pl
from jax.experimental.pallas import tpu as pltpu
from jax.sharding import PartitionSpec as P

MESH = pl.DeviceIdType.MESH
F32, BF16 = jnp.float32, jnp.bfloat16

NY, NZ, NX = 4, 8, 4
GROUPS = NY * NZ
TOK, TOP, CAP = 64, 8, 24
FEAT, HPART = 896, 256
DEV = 2 * NX
ROWS = GROUPS * CAP
CHUNKS = NZ
CROWS = NY * CAP
HALF = CROWS // 2
DISTANCE = (1, 7, 4, 3, 5, 2, 6, 0)
AHEAD = 2

RIGHT, LEFT, RIGHT2, LEFT2, SIB_OWN, SIB_LEFT, SIB_RIGHT, SIB_FAR = range(8)


def distance_of(chunk):
    found = 0
    for index, value in enumerate(DISTANCE):
        if value:
            found = found + jnp.where(chunk == index, value, 0)
    return found


def kernel(
    tokens_ref, routes_ref, affinity_ref, gate_hbm, up_hbm, down_hbm, out_ref,
    gate_ref, up_ref, down_ref, outgoing, landed, rows, hidden, results, returned, weight_of, total,
    weight_sem, self_sem, sent_sem, landed_sem, back_sem, returned_sem, x_send, x_recv, h_send, h_recv,
):
    me_g, me_l = lax.axis_index("group"), lax.axis_index("local")
    y, z = me_g // NZ, lax.rem(me_g, NZ)
    x, core = me_l // 2, lax.rem(me_l, 2)
    right = lax.rem(x + 1, NX) * 2 + core
    left = lax.rem(x + NX - 1, NX) * 2 + core
    far = lax.rem(x + 2, NX) * 2 + core
    sibling = x * 2 + 1 - core

    def group_at(dy, dz):
        return lax.rem(y + dy, NY) * NZ + lax.rem(z + dz, NZ)

    barrier = pltpu.get_barrier_semaphore()

    def greet(offset, carry):
        pl.semaphore_signal(
            barrier, inc=1, device_id=(lax.rem(me_g + offset, GROUPS), me_l), device_id_type=MESH
        )
        return carry

    lax.fori_loop(1, GROUPS, greet, 0)
    for peer in (right, left, sibling):
        pl.semaphore_signal(barrier, inc=1, device_id=(me_g, peer), device_id_type=MESH)

    weights = [
        pltpu.make_async_copy(source.at[0], target, weight_sem.at[index])
        for index, (source, target) in enumerate(
            ((gate_hbm, gate_ref), (up_hbm, up_ref), (down_hbm, down_ref))
        )
    ]
    for copy in weights:
        copy.start()

    block = lax.broadcasted_iota(jnp.int32, (GROUPS, TOK), 0)
    dz_of = distance_of(block // NY)
    dy_of = block - (block // NY) * NY
    yy, zz = y + NY - dy_of, z + NZ - dz_of
    yy = jnp.where(yy >= NY, yy - NY, yy)
    zz = jnp.where(zz >= NZ, zz - NZ, zz)
    expert = yy * NZ + zz
    named = jnp.zeros((GROUPS, TOK), F32)
    gates = jnp.zeros((GROUPS, TOK), F32)
    for k in range(TOP):
        same = routes_ref[k : k + 1, :] == expert
        named = named + jnp.where(same, 1.0, 0.0)
        gates = gates + jnp.where(same, affinity_ref[k : k + 1, :], 0.0)
    before = lax.broadcasted_iota(jnp.int32, (TOK, TOK), 0) < lax.broadcasted_iota(jnp.int32, (TOK, TOK), 1)
    earlier = jnp.dot(named.astype(BF16), jnp.where(before, 1.0, 0.0).astype(BF16), preferred_element_type=F32)
    slot = jnp.where(named > 0.5, earlier, -1.0).astype(jnp.int32)
    place = lax.broadcasted_iota(jnp.int32, (GROUPS, CAP, TOK), 1)
    holds = slot[:, None, :] == place
    pick = jnp.where(holds, 1.0, 0.0).reshape(ROWS, TOK).astype(BF16)
    for at in range(0, GROUPS, 8):
        part = jnp.dot(pick[at * CAP : (at + 8) * CAP], tokens_ref[...], preferred_element_type=F32)
        outgoing[at : at + 8] = part.reshape(8, CAP, FEAT).astype(BF16)

    pl.semaphore_wait(barrier, GROUPS - 1 + 3)

    own = DISTANCE.index(0) * NY
    own_chunk = own // NY
    self_copy = pltpu.make_async_copy(outgoing.at[own], landed.at[own], self_sem.at[0])
    self_copy.start()

    def dispatch(s, carry):
        dz, dy = distance_of(s // NY), lax.rem(s, NY)

        @pl.when(s != own)
        def _():
            pltpu.make_async_remote_copy(
                src_ref=outgoing.at[s],
                dst_ref=landed.at[s],
                send_sem=sent_sem.at[0],
                recv_sem=landed_sem.at[s],
                device_id=(group_at(NY - dy, NZ - dz), me_l),
                device_id_type=MESH,
            ).start()

        return carry

    lax.fori_loop(0, GROUPS, dispatch, 0)

    spread = jnp.where(holds, gates[:, None, :], 0.0).reshape(ROWS, TOK)
    high = spread.astype(BF16)
    low = (spread - high.astype(F32)).astype(BF16)
    weight_of[...] = jnp.concatenate([high.astype(F32), low.astype(F32)], axis=1).reshape(
        CHUNKS, CROWS, 2 * TOK
    )
    total[...] = jnp.zeros_like(total)

    def ring(buffer, send, recv, kind, chunk):
        start = pl.multiple_of(chunk * CROWS, CROWS)
        slot_of, begin, count, target = {
            RIGHT: (me_l, 0, CROWS, right),
            LEFT: (me_l, 0, CROWS, left),
            RIGHT2: (left, 0, HALF, right),
            LEFT2: (right, HALF, HALF, left),
            SIB_OWN: (me_l, 0, CROWS, sibling),
            SIB_LEFT: (left, 0, CROWS, sibling),
            SIB_RIGHT: (right, 0, CROWS, sibling),
            SIB_FAR: (far, 0, CROWS, sibling),
        }[kind]
        piece = buffer.at[slot_of, pl.ds(start + begin, count)]
        return pltpu.make_async_remote_copy(
            src_ref=piece,
            dst_ref=piece,
            send_sem=send.at[kind, chunk],
            recv_sem=recv.at[kind, chunk],
            device_id=(me_g, target),
            device_id_type=MESH,
        )

    def x_ring(kind, chunk):
        return ring(rows, x_send, x_recv, kind, chunk)

    def h_ring(kind, chunk):
        return ring(hidden, h_send, h_recv, kind, chunk)

    def begin_rows(chunk):
        for dy in range(NY):
            s = chunk * NY + dy

            @pl.when(s != own)
            def _():
                pltpu.make_async_copy(landed.at[s], landed.at[s], landed_sem.at[s]).wait()

            if dy == 0:

                @pl.when(s == own)
                def _():
                    self_copy.wait()

        blocks = landed[pl.ds(chunk * NY, NY)].astype(F32).reshape(CROWS, FEAT).astype(BF16)
        rows[me_l, pl.ds(pl.multiple_of(chunk * CROWS, CROWS), CROWS)] = blocks
        for kind in (RIGHT, LEFT, SIB_OWN):
            x_ring(kind, chunk).start()

    def second(make, chunk):
        make(RIGHT, chunk).wait_recv()
        make(RIGHT2, chunk).start()
        make(SIB_LEFT, chunk).start()
        make(LEFT, chunk).wait_recv()
        make(LEFT2, chunk).start()
        make(SIB_RIGHT, chunk).start()

    def third(make, chunk):
        make(RIGHT2, chunk).wait_recv()
        make(LEFT2, chunk).wait_recv()
        make(SIB_FAR, chunk).start()

    def gathered(make, chunk):
        for kind in (SIB_OWN, SIB_LEFT, SIB_RIGHT, SIB_FAR):
            make(kind, chunk).wait_recv()

    def hidden_rows(chunk):
        here = pl.ds(pl.multiple_of(chunk * CROWS, CROWS), CROWS)
        gate = jnp.zeros((CROWS, HPART), F32)
        up = jnp.zeros((CROWS, HPART), F32)
        for pair in range(NX):
            lhs = jnp.concatenate([rows[2 * pair, here], rows[2 * pair + 1, here]], axis=1)
            depth = slice(pair * 2 * FEAT, (pair + 1) * 2 * FEAT)
            gate = gate + jnp.dot(lhs, gate_ref[depth, :], preferred_element_type=F32)
            up = up + jnp.dot(lhs, up_ref[depth, :], preferred_element_type=F32)
        value = gate / (1.0 + jnp.exp(-gate)) * up
        hidden[me_l, here] = value.astype(BF16)

    def output_rows(chunk):
        here = pl.ds(pl.multiple_of(chunk * CROWS, CROWS), CROWS)
        lhs = jnp.concatenate([hidden[part, here] for part in range(DEV)], axis=1)
        value = jnp.dot(lhs, down_ref[...], preferred_element_type=F32)
        results[pl.ds(chunk * NY, NY)] = value.reshape(NY, CAP, FEAT).astype(BF16)

    def send_back(chunk):
        dz = distance_of(chunk)
        for dy in range(NY):
            s = chunk * NY + dy

            @pl.when(s != own)
            def _():
                pltpu.make_async_remote_copy(
                    src_ref=results.at[s],
                    dst_ref=returned.at[s],
                    send_sem=back_sem.at[0],
                    recv_sem=returned_sem.at[s],
                    device_id=(group_at(dy, dz), me_l),
                    device_id_type=MESH,
                ).start()

            if dy == 0:

                @pl.when(s == own)
                def _():
                    pltpu.make_async_copy(results.at[s], returned.at[s], self_sem.at[1]).start()

    def combine(chunk):
        for dy in range(NY):
            s = chunk * NY + dy

            @pl.when(s != own)
            def _():
                pltpu.make_async_copy(returned.at[s], returned.at[s], returned_sem.at[s]).wait()

            if dy == 0:

                @pl.when(s == own)
                def _():
                    pltpu.make_async_copy(results.at[s], returned.at[s], self_sem.at[1]).wait()

        values = returned[pl.ds(chunk * NY, NY)].astype(F32).reshape(CROWS, FEAT).astype(BF16)
        both = lax.dot_general(
            weight_of[chunk].astype(BF16), values, (((0,), (0,)), ((), ())), preferred_element_type=F32
        )
        total[...] += both[:TOK] + both[TOK:]

    def early(chunk, carry):
        begin_rows(chunk)
        return carry

    lax.fori_loop(0, AHEAD, early, 0)

    def turn(i, carry):
        @pl.when(i < CHUNKS)
        def _():
            second(x_ring, i)

        @pl.when(i + AHEAD < CHUNKS)
        def _():
            begin_rows(i + AHEAD)

        @pl.when(i >= 1)
        def _():
            second(h_ring, i - 1)

        @pl.when(i < CHUNKS)
        def _():
            third(x_ring, i)

        @pl.when(i >= 1)
        def _():
            third(h_ring, i - 1)

        @pl.when(i == 0)
        def _():
            weights[0].wait()
            weights[1].wait()

        @pl.when(i < CHUNKS)
        def _():
            gathered(x_ring, i)
            hidden_rows(i)
            for kind in (RIGHT, LEFT, SIB_OWN):
                h_ring(kind, i).start()

        @pl.when(i == 1)
        def _():
            weights[2].wait()

        @pl.when(i >= 1)
        def _():
            gathered(h_ring, i - 1)
            output_rows(i - 1)
            send_back(i - 1)

        return carry

    lax.fori_loop(0, CHUNKS + 1, turn, 0)

    def collect(chunk, carry):
        combine(chunk)
        return carry

    lax.fori_loop(0, CHUNKS, collect, 0)
    out_ref[...] = total[...].astype(BF16)

    def settle(chunk, carry):
        for kind in range(8):
            x_ring(kind, chunk).wait_send()
            h_ring(kind, chunk).wait_send()
        return carry

    lax.fori_loop(0, CHUNKS, settle, 0)
    others = pl.ds(0, GROUPS - 1)
    pltpu.make_async_copy(outgoing.at[others], outgoing.at[others], sent_sem.at[0]).wait()
    pltpu.make_async_copy(results.at[others], results.at[others], back_sem.at[0]).wait()


def on_device(tokens, routes, affinity, gate_proj, up_proj, down_proj):
    vmem, anywhere = pl.BlockSpec(memory_space=pltpu.VMEM), pl.BlockSpec(memory_space=pl.ANY)
    dma = pltpu.SemaphoreType.DMA
    return pl.pallas_call(
        kernel,
        out_shape=jax.ShapeDtypeStruct((TOK, FEAT), BF16),
        in_specs=[vmem, vmem, vmem, anywhere, anywhere, anywhere],
        out_specs=vmem,
        scratch_shapes=[
            pltpu.VMEM((DEV * FEAT, HPART), BF16),
            pltpu.VMEM((DEV * FEAT, HPART), BF16),
            pltpu.VMEM((DEV * HPART, FEAT), BF16),
            pltpu.VMEM((GROUPS, CAP, FEAT), BF16),
            pltpu.VMEM((GROUPS, CAP, FEAT), BF16),
            pltpu.VMEM((DEV, ROWS, FEAT), BF16),
            pltpu.VMEM((DEV, ROWS, HPART), BF16),
            pltpu.VMEM((GROUPS, CAP, FEAT), BF16),
            pltpu.VMEM((GROUPS, CAP, FEAT), BF16),
            pltpu.VMEM((CHUNKS, CROWS, 2 * TOK), F32),
            pltpu.VMEM((TOK, FEAT), F32),
            dma((3,)),
            dma((2,)),
            dma((1,)),
            dma((GROUPS,)),
            dma((1,)),
            dma((GROUPS,)),
            dma((8, CHUNKS)),
            dma((8, CHUNKS)),
            dma((8, CHUNKS)),
            dma((8, CHUNKS)),
        ],
        compiler_params=pltpu.CompilerParams(
            collective_id=0, has_side_effects=True, vmem_limit_bytes=56 * 1024 * 1024
        ),
        cost_estimate=pl.CostEstimate(flops=8_500_000_000, bytes_accessed=11_500_000, transcendentals=200_000),
    )(tokens, routes.T, affinity.T, gate_proj, up_proj, down_proj)


def solution(mesh):
    in_specs = (
        P("group", "local"),
        P("group", None),
        P("group", None),
        P("group", None, "local"),
        P("group", None, "local"),
        P("group", None, "local"),
    )
    return jax.shard_map(
        on_device, mesh=mesh, in_specs=in_specs, out_specs=P("group", "local"), check_vma=False
    )
```

time: 233 us -> 128 us (0.55)
  the two profiles are of different devices: /device:TPU:97 before, /device:TPU:35 now
where the time goes in v1:
time: 128 us
  Pallas kernels  126 us (98%)
  local copies, waits for them, and re-layouts  1.55 us (1%)
    pallas_call x1, Pallas kernels, on_device(): pl.pallas_call(kernel, out_shape=jax.ShapeDtypeStruct((TOK, FEAT), BF16),...  126 us

profile of v1, /device:TPU:35, one launch (start us, length us, event | category | flops | bytes accessed | tf_op | source)
XLA Modules:
  0.0 128.0 jit_solution(16869248758380876301)
XLA Ops:
  0.0 126.4 %shard_map.64 = bf16[64,896]{1,0:T(8,128)(2,1)} custom-call(bf16[64,896]{1,0:T(8,128)(2,1)} %tokens_ref.1, s32[8,64]{1,0:T(8,128)} %bitcast.2, f32[8,64]{1,0:T(8,128)} %bitcast.3, bf16[1,7168,256]{2,1,0:T(8,128)(2,1)} %gate_hbm.1, bf16[1,7168,256]{2,1,0:T(8,128)(2,1)} %up_hbm.1, bf16[1,2048,896]{2,1,0:T(8,128)(2,1)} %down_hbm.1), custom_call_target="tpu_custom_call" | custom-call | flops 8499999744 | bytes 11500000 | tf_op jit(solution)/shard_map/pallas_call | solution.py:326
  126.4 1.6 %copy.8 = bf16[64,896]{1,0:T(8,128)(2,1)} copy(bf16[64,896]{1,0:T(8,128)(2,1)} %shard_map.64) | data formatting | bytes 229376

commit v2 on v1

--- a/solution.py
+++ b/solution.py
@@ -44,18 +44,17 @@
     far = lax.rem(x + 2, NX) * 2 + core
     sibling = x * 2 + 1 - core
 
+    def wrap(value, size):
+        return jnp.where(value >= size, value - size, value)
+
     def group_at(dy, dz):
-        return lax.rem(y + dy, NY) * NZ + lax.rem(z + dz, NZ)
+        return wrap(y + dy, NY) * NZ + wrap(z + dz, NZ)
 
     barrier = pltpu.get_barrier_semaphore()
-
-    def greet(offset, carry):
+    for offset in range(1, GROUPS):
         pl.semaphore_signal(
-            barrier, inc=1, device_id=(lax.rem(me_g + offset, GROUPS), me_l), device_id_type=MESH
+            barrier, inc=1, device_id=(wrap(me_g + offset, GROUPS), me_l), device_id_type=MESH
         )
-        return carry
-
-    lax.fori_loop(1, GROUPS, greet, 0)
     for peer in (right, left, sibling):
         pl.semaphore_signal(barrier, inc=1, device_id=(me_g, peer), device_id_type=MESH)
 
@@ -108,7 +107,7 @@
                 dst_ref=landed.at[s],
                 send_sem=sent_sem.at[0],
                 recv_sem=landed_sem.at[s],
-                device_id=(group_at(NY - dy, NZ - dz), me_l),
+                device_id=(group_at(NY - dy - jnp.where(dy == 0, NY, 0), NZ - dz - jnp.where(dz == 0, NZ, 0)), me_l),
                 device_id_type=MESH,
             ).start()
 
@@ -263,43 +262,43 @@
         def _():
             begin_rows(i + AHEAD)
 
-        @pl.when(i >= 1)
-        def _():
-            second(h_ring, i - 1)
-
-        @pl.when(i < CHUNKS)
-        def _():
-            third(x_ring, i)
-
-        @pl.when(i >= 1)
-        def _():
-            third(h_ring, i - 1)
-
-        @pl.when(i == 0)
+        @pl.when((i >= 1) & (i < CHUNKS + 1))
+        def _():
+            third(x_ring, i - 1)
+
+        @pl.when((i >= 2) & (i < CHUNKS + 2))
+        def _():
+            second(h_ring, i - 2)
+
+        @pl.when(i >= 3)
+        def _():
+            third(h_ring, i - 3)
+
+        @pl.when(i == 1)
         def _():
             weights[0].wait()
             weights[1].wait()
 
-        @pl.when(i < CHUNKS)
-        def _():
-            gathered(x_ring, i)
-            hidden_rows(i)
+        @pl.when((i >= 1) & (i < CHUNKS + 1))
+        def _():
+            gathered(x_ring, i - 1)
+            hidden_rows(i - 1)
             for kind in (RIGHT, LEFT, SIB_OWN):
-                h_ring(kind, i).start()
-
-        @pl.when(i == 1)
+                h_ring(kind, i - 1).start()
+
+        @pl.when(i == 3)
         def _():
             weights[2].wait()
 
-        @pl.when(i >= 1)
-        def _():
-            gathered(h_ring, i - 1)
-            output_rows(i - 1)
-            send_back(i - 1)
-
-        return carry
-
-    lax.fori_loop(0, CHUNKS + 1, turn, 0)
+        @pl.when(i >= 3)
+        def _():
+            gathered(h_ring, i - 3)
+            output_rows(i - 3)
+            send_back(i - 3)
+
+        return carry
+
+    lax.fori_loop(0, CHUNKS + 3, turn, 0)
 
     def collect(chunk, carry):
         combine(chunk)

time: 128 us -> 107 us (0.84)
  the two profiles are of different devices: /device:TPU:35 before, /device:TPU:1 now
where the time goes in v2:
time: 107 us
  Pallas kernels  105 us (98%)
  local copies, waits for them, and re-layouts  1.55 us (1%)
    pallas_call x1, Pallas kernels, on_device(): pl.pallas_call(kernel, out_shape=jax.ShapeDtypeStruct((TOK, FEAT), BF16),...  105 us

profile of v2, /device:TPU:1, one launch (start us, length us, event | category | flops | bytes accessed | tf_op | source)
XLA Modules:
  0.0 106.9 jit_solution(389904663528238220)
XLA Ops:
  0.0 105.4 %shard_map.64 = bf16[64,896]{1,0:T(8,128)(2,1)} custom-call(bf16[64,896]{1,0:T(8,128)(2,1)} %tokens_ref.1, s32[8,64]{1,0:T(8,128)} %bitcast.2, f32[8,64]{1,0:T(8,128)} %bitcast.3, bf16[1,7168,256]{2,1,0:T(8,128)(2,1)} %gate_hbm.1, bf16[1,7168,256]{2,1,0:T(8,128)(2,1)} %up_hbm.1, bf16[1,2048,896]{2,1,0:T(8,128)(2,1)} %down_hbm.1), custom_call_target="tpu_custom_call" | custom-call | flops 8499999744 | bytes 11500000 | tf_op jit(solution)/shard_map/pallas_call | solution.py:325
  105.4 1.6 %copy.8 = bf16[64,896]{1,0:T(8,128)(2,1)} copy(bf16[64,896]{1,0:T(8,128)(2,1)} %shard_map.64) | data formatting | bytes 229376

commit v3 on v2

v3 whole, which is shorter than its diff:
```python
import jax
import jax.numpy as jnp
from jax import lax
from jax.experimental import pallas as pl
from jax.experimental.pallas import tpu as pltpu
from jax.sharding import PartitionSpec as P

MESH = pl.DeviceIdType.MESH
F32, BF16 = jnp.float32, jnp.bfloat16

NY, NZ, NX = 4, 8, 4
GROUPS = NY * NZ
TOK, TOP, CAP = 64, 8, 24
FEAT, HPART = 896, 256
DEV = 2 * NX
ROWS = GROUPS * CAP
CHUNKS = NZ
CROWS = NY * CAP
HALF = CROWS // 2
DISTANCE = (1, 7, 4, 3, 5, 2, 6, 0)
AHEAD = 2

RIGHT, LEFT, RIGHT2, LEFT2, SIBLING = range(5)
FAR = RIGHT2


def distance_of(chunk):
    found = 0
    for index, value in enumerate(DISTANCE):
        if value:
            found = found + jnp.where(chunk == index, value, 0)
    return found


def kernel(
    tokens_ref, routes_ref, affinity_ref, gate_hbm, up_hbm, down_hbm, out_ref,
    gate_ref, up_ref, down_ref, outgoing, landed, rows, hidden, results, returned, weight_of, total,
    weight_sem, sent_sem, landed_sem, back_sem, returned_sem, x_send, x_recv, h_send, h_recv,
):
    me_g, me_l = lax.axis_index("group"), lax.axis_index("local")
    y, z = me_g // NZ, lax.rem(me_g, NZ)
    x, core = me_l // 2, lax.rem(me_l, 2)
    right = lax.rem(x + 1, NX) * 2 + core
    left = lax.rem(x + NX - 1, NX) * 2 + core
    right_x, left_x, far_x = lax.rem(x + 1, NX), lax.rem(x + NX - 1, NX), lax.rem(x + 2, NX)
    sibling = x * 2 + 1 - core

    def wrap(value, size):
        return jnp.where(value >= size, value - size, value)

    def group_at(dy, dz):
        return wrap(y + dy, NY) * NZ + wrap(z + dz, NZ)

    barrier = pltpu.get_barrier_semaphore()
    for offset in range(1, GROUPS):
        pl.semaphore_signal(
            barrier, inc=1, device_id=(wrap(me_g + offset, GROUPS), me_l), device_id_type=MESH
        )
    for peer in (right, left, sibling):
        pl.semaphore_signal(barrier, inc=1, device_id=(me_g, peer), device_id_type=MESH)

    weights = [
        pltpu.make_async_copy(source.at[0], target, weight_sem.at[index])
        for index, (source, target) in enumerate(
            ((gate_hbm, gate_ref), (up_hbm, up_ref), (down_hbm, down_ref))
        )
    ]
    for copy in weights:
        copy.start()

    block = lax.broadcasted_iota(jnp.int32, (GROUPS, TOK), 0)
    dz_of = distance_of(block // NY)
    dy_of = block - (block // NY) * NY
    yy, zz = y + NY - dy_of, z + NZ - dz_of
    yy = jnp.where(yy >= NY, yy - NY, yy)
    zz = jnp.where(zz >= NZ, zz - NZ, zz)
    expert = yy * NZ + zz
    named = jnp.zeros((GROUPS, TOK), F32)
    gates = jnp.zeros((GROUPS, TOK), F32)
    for k in range(TOP):
        same = routes_ref[k : k + 1, :] == expert
        named = named + jnp.where(same, 1.0, 0.0)
        gates = gates + jnp.where(same, affinity_ref[k : k + 1, :], 0.0)
    before = lax.broadcasted_iota(jnp.int32, (TOK, TOK), 0) < lax.broadcasted_iota(jnp.int32, (TOK, TOK), 1)
    earlier = jnp.dot(named.astype(BF16), jnp.where(before, 1.0, 0.0).astype(BF16), preferred_element_type=F32)
    slot = jnp.where(named > 0.5, earlier, -1.0).astype(jnp.int32)
    place = lax.broadcasted_iota(jnp.int32, (GROUPS, CAP, TOK), 1)
    holds = slot[:, None, :] == place
    pick = jnp.where(holds, 1.0, 0.0).reshape(ROWS, TOK).astype(BF16)
    for at in range(0, GROUPS, 8):
        part = jnp.dot(pick[at * CAP : (at + 8) * CAP], tokens_ref[...], preferred_element_type=F32)
        outgoing[at : at + 8] = part.reshape(8, CAP, FEAT).astype(BF16)

    pl.semaphore_wait(barrier, GROUPS - 1 + 3)

    own = DISTANCE.index(0) * NY
    pltpu.make_async_copy(outgoing.at[own], landed.at[own], landed_sem.at[own // NY]).start()

    def dispatch(s, carry):
        dz, dy = distance_of(s // NY), lax.rem(s, NY)

        @pl.when(s != own)
        def _():
            pltpu.make_async_remote_copy(
                src_ref=outgoing.at[s],
                dst_ref=landed.at[s],
                send_sem=sent_sem.at[0],
                recv_sem=landed_sem.at[s // NY],
                device_id=(group_at(NY - dy - jnp.where(dy == 0, NY, 0), NZ - dz - jnp.where(dz == 0, NZ, 0)), me_l),
                device_id_type=MESH,
            ).start()

        return carry

    lax.fori_loop(0, GROUPS, dispatch, 0)

    spread = jnp.where(holds, gates[:, None, :], 0.0).reshape(ROWS, TOK)
    high = spread.astype(BF16)
    low = (spread - high.astype(F32)).astype(BF16)
    weight_of[...] = jnp.concatenate([high.astype(F32), low.astype(F32)], axis=1).reshape(
        CHUNKS, CROWS, 2 * TOK
    )
    total[...] = jnp.zeros_like(total)

    def ring(buffer, send, recv, kind, chunk):
        start = pl.multiple_of(chunk * CROWS, CROWS)
        slots, begin, count, target = {
            RIGHT: (x, 0, CROWS, right),
            LEFT: (x, 0, CROWS, left),
            RIGHT2: (left_x, 0, HALF, right),
            LEFT2: (right_x, HALF, HALF, left),
            SIBLING: (pl.ds(0, NX), 0, CROWS, sibling),
        }[kind]
        piece = buffer.at[core, slots, pl.ds(start + begin, count)]
        return pltpu.make_async_remote_copy(
            src_ref=piece,
            dst_ref=piece,
            send_sem=send.at[kind],
            recv_sem=recv.at[FAR if kind == LEFT2 else kind, chunk],
            device_id=(me_g, target),
            device_id_type=MESH,
        )

    def arrival(buffer, recv, kind, chunk):
        here = pl.ds(pl.multiple_of(chunk * CROWS, CROWS), CROWS)
        piece = {
            RIGHT: lambda: buffer.at[core, left_x, here],
            LEFT: lambda: buffer.at[core, right_x, here],
            FAR: lambda: buffer.at[core, far_x, here],
            SIBLING: lambda: buffer.at[1 - core, pl.ds(0, NX), here],
        }[kind]()
        pltpu.make_async_copy(piece, piece, recv.at[kind, chunk]).wait()

    x_ring, h_ring = (rows, x_send, x_recv), (hidden, h_send, h_recv)

    def begin_rows(chunk):
        blocks_of = landed.at[pl.ds(chunk * NY, NY)]
        pltpu.make_async_copy(blocks_of, blocks_of, landed_sem.at[chunk]).wait()
        blocks = blocks_of[...].astype(F32).reshape(CROWS, FEAT).astype(BF16)
        rows[core, x, pl.ds(pl.multiple_of(chunk * CROWS, CROWS), CROWS)] = blocks
        for kind in (RIGHT, LEFT):
            ring(*x_ring, kind, chunk).start()

    def second(kit, chunk):
        for kind, onward in ((RIGHT, RIGHT2), (LEFT, LEFT2)):
            arrival(kit[0], kit[2], kind, chunk)
            ring(*kit, onward, chunk).start()

    def third(kit, chunk):
        arrival(kit[0], kit[2], FAR, chunk)
        ring(*kit, SIBLING, chunk).start()

    def gathered(kit, chunk):
        arrival(kit[0], kit[2], SIBLING, chunk)

    def hidden_rows(chunk):
        here = pl.ds(pl.multiple_of(chunk * CROWS, CROWS), CROWS)
        gate = jnp.zeros((CROWS, HPART), F32)
        up = jnp.zeros((CROWS, HPART), F32)
        for pair in range(NX):
            lhs = jnp.concatenate([rows[0, pair, here], rows[1, pair, here]], axis=1)
            depth = slice(pair * 2 * FEAT, (pair + 1) * 2 * FEAT)
            gate = gate + jnp.dot(lhs, gate_ref[depth, :], preferred_element_type=F32)
            up = up + jnp.dot(lhs, up_ref[depth, :], preferred_element_type=F32)
        value = gate / (1.0 + jnp.exp(-gate)) * up
        hidden[core, x, here] = value.astype(BF16)

    def output_rows(chunk):
        here = pl.ds(pl.multiple_of(chunk * CROWS, CROWS), CROWS)
        lhs = jnp.concatenate([hidden[part % 2, part // 2, here] for part in range(DEV)], axis=1)
        value = jnp.dot(lhs, down_ref[...], preferred_element_type=F32)
        results[pl.ds(chunk * NY, NY)] = value.reshape(NY, CAP, FEAT).astype(BF16)

    def send_back(chunk):
        dz = distance_of(chunk)
        for dy in range(NY):
            s = chunk * NY + dy

            @pl.when(s != own)
            def _():
                pltpu.make_async_remote_copy(
                    src_ref=results.at[s],
                    dst_ref=returned.at[s],
                    send_sem=back_sem.at[0],
                    recv_sem=returned_sem.at[chunk],
                    device_id=(group_at(dy, dz), me_l),
                    device_id_type=MESH,
                ).start()

            if dy == 0:

                @pl.when(s == own)
                def _():
                    pltpu.make_async_copy(results.at[s], returned.at[s], returned_sem.at[chunk]).start()

    def combine(chunk):
        blocks_of = returned.at[pl.ds(chunk * NY, NY)]
        pltpu.make_async_copy(blocks_of, blocks_of, returned_sem.at[chunk]).wait()
        values = blocks_of[...].astype(F32).reshape(CROWS, FEAT).astype(BF16)
        both = lax.dot_general(
            weight_of[chunk].astype(BF16), values, (((0,), (0,)), ((), ())), preferred_element_type=F32
        )
        total[...] += both[:TOK] + both[TOK:]

    def early(chunk, carry):
        begin_rows(chunk)
        return carry

    lax.fori_loop(0, AHEAD, early, 0)

    def turn(i, carry):
        @pl.when((i >= 1) & (i < CHUNKS + 1))
        def _():
            third(x_ring, i - 1)

        @pl.when(i >= 3)
        def _():
            third(h_ring, i - 3)

        @pl.when(i < CHUNKS)
        def _():
            second(x_ring, i)

        @pl.when(i + AHEAD < CHUNKS)
        def _():
            begin_rows(i + AHEAD)

        @pl.when(i == 3)
        def _():
            weights[2].wait()

        @pl.when(i >= 3)
        def _():
            gathered(h_ring, i - 3)
            output_rows(i - 3)
            send_back(i - 3)

        @pl.when((i >= 2) & (i < CHUNKS + 2))
        def _():
            second(h_ring, i - 2)

        @pl.when(i == 1)
        def _():
            weights[0].wait()
            weights[1].wait()

        @pl.when((i >= 1) & (i < CHUNKS + 1))
        def _():
            gathered(x_ring, i - 1)
            hidden_rows(i - 1)
            for kind in (RIGHT, LEFT):
                ring(*h_ring, kind, i - 1).start()

        return carry

    lax.fori_loop(0, CHUNKS + 3, turn, 0)

    def collect(chunk, carry):
        combine(chunk)
        return carry

    lax.fori_loop(0, CHUNKS, collect, 0)
    out_ref[...] = total[...].astype(BF16)

    for buffer, send, _ in (x_ring, h_ring):
        for kind, piece in (
            (RIGHT, buffer.at[core, x]),
            (LEFT, buffer.at[core, x]),
            (RIGHT2, buffer.at[core, left_x, pl.ds(0, ROWS // 2)]),
            (LEFT2, buffer.at[core, right_x, pl.ds(0, ROWS // 2)]),
            (SIBLING, buffer.at[core]),
        ):
            pltpu.make_async_copy(piece, piece, send.at[kind]).wait()
    others = pl.ds(0, GROUPS - 1)
    pltpu.make_async_copy(outgoing.at[others], outgoing.at[others], sent_sem.at[0]).wait()
    pltpu.make_async_copy(results.at[others], results.at[others], back_sem.at[0]).wait()


def on_device(tokens, routes, affinity, gate_proj, up_proj, down_proj):
    vmem, anywhere = pl.BlockSpec(memory_space=pltpu.VMEM), pl.BlockSpec(memory_space=pl.ANY)
    dma = pltpu.SemaphoreType.DMA
    return pl.pallas_call(
        kernel,
        out_shape=pltpu.VMEM((TOK, FEAT), BF16),
        in_specs=[vmem, vmem, vmem, anywhere, anywhere, anywhere],
        out_specs=vmem,
        scratch_shapes=[
            pltpu.VMEM((DEV * FEAT, HPART), BF16),
            pltpu.VMEM((DEV * FEAT, HPART), BF16),
            pltpu.VMEM((DEV * HPART, FEAT), BF16),
            pltpu.VMEM((GROUPS, CAP, FEAT), BF16),
            pltpu.VMEM((GROUPS, CAP, FEAT), BF16),
            pltpu.VMEM((2, NX, ROWS, FEAT), BF16),
            pltpu.VMEM((2, NX, ROWS, HPART), BF16),
            pltpu.VMEM((GROUPS, CAP, FEAT), BF16),
            pltpu.VMEM((GROUPS, CAP, FEAT), BF16),
            pltpu.VMEM((CHUNKS, CROWS, 2 * TOK), F32),
            pltpu.VMEM((TOK, FEAT), F32),
            dma((3,)),
            dma((1,)),
            dma((CHUNKS,)),
            dma((1,)),
            dma((CHUNKS,)),
            dma((5,)),
            dma((5, CHUNKS)),
            dma((5,)),
            dma((5, CHUNKS)),
        ],
        compiler_params=pltpu.CompilerParams(
            collective_id=0, has_side_effects=True, vmem_limit_bytes=56 * 1024 * 1024
        ),
        cost_estimate=pl.CostEstimate(flops=8_500_000_000, bytes_accessed=11_500_000, transcendentals=200_000),
    )(tokens, routes.T, affinity.T, gate_proj, up_proj, down_proj)


def solution(mesh):
    in_specs = (
        P("group", "local"),
        P("group", None),
        P("group", None),
        P("group", None, "local"),
        P("group", None, "local"),
        P("group", None, "local"),
    )
    return jax.shard_map(
        on_device, mesh=mesh, in_specs=in_specs, out_specs=P("group", "local"), check_vma=False
    )
```

time: 107 us -> 105 us (0.981)
  the two profiles are of different devices: /device:TPU:1 before, /device:TPU:97 now
where the time goes in v3:
time: 105 us; the launch traced here: 103 us
  Pallas kernels  103 us (98%)
    pallas_call x1, Pallas kernels, on_device(): pl.pallas_call(kernel, out_shape=pltpu.VMEM((TOK, FEAT), BF16), in_specs=...  103 us

profile of v3, /device:TPU:97, one launch (start us, length us, event | category | flops | bytes accessed | tf_op | source)
XLA Modules:
  0.0 103.4 jit_solution(17299260331872849331)
XLA Ops:
  0.0 102.8 %shard_map.64 = bf16[64,896]{1,0:T(8,128)(2,1)S(1)} custom-call(bf16[64,896]{1,0:T(8,128)(2,1)} %tokens_ref.1, s32[8,64]{1,0:T(8,128)} %bitcast.2, f32[8,64]{1,0:T(8,128)} %bitcast.3, bf16[1,7168,256]{2,1,0:T(8,128)(2,1)} %gate_hbm.1, bf16[1,7168,256]{2,1,0:T(8,128)(2,1)} %up_hbm.1, bf16[1,2048,896]{2,1,0:T(8,128)(2,1)} %down_hbm.1), custom_call_target="tpu_custom_call" | custom-call | flops 8499999744 | bytes 11500000 | tf_op jit(solution)/shard_map/pallas_call | solution.py:302
  102.8 0.6 copy.8

commit v4 on v3

--- a/solution.py
+++ b/solution.py
@@ -17,10 +17,10 @@
 CHUNKS = NZ
 CROWS = NY * CAP
 HALF = CROWS // 2
-DISTANCE = (1, 7, 4, 3, 5, 2, 6, 0)
+DISTANCE = (1, 7, 2, 6, 3, 5, 4, 0)
 AHEAD = 2
 
-RIGHT, LEFT, RIGHT2, LEFT2, SIBLING = range(5)
+RIGHT, LEFT, RIGHT2, LEFT2, SIBLING, OVER = range(6)
 FAR = RIGHT2
 
 
@@ -42,6 +42,7 @@
     x, core = me_l // 2, lax.rem(me_l, 2)
     right = lax.rem(x + 1, NX) * 2 + core
     left = lax.rem(x + NX - 1, NX) * 2 + core
+    far = lax.rem(x + 2, NX) * 2 + core
     right_x, left_x, far_x = lax.rem(x + 1, NX), lax.rem(x + NX - 1, NX), lax.rem(x + 2, NX)
     sibling = x * 2 + 1 - core
 
@@ -56,7 +57,7 @@
         pl.semaphore_signal(
             barrier, inc=1, device_id=(wrap(me_g + offset, GROUPS), me_l), device_id_type=MESH
         )
-    for peer in (right, left, sibling):
+    for peer in (right, left, far, sibling):
         pl.semaphore_signal(barrier, inc=1, device_id=(me_g, peer), device_id_type=MESH)
 
     weights = [
@@ -91,7 +92,7 @@
         part = jnp.dot(pick[at * CAP : (at + 8) * CAP], tokens_ref[...], preferred_element_type=F32)
         outgoing[at : at + 8] = part.reshape(8, CAP, FEAT).astype(BF16)
 
-    pl.semaphore_wait(barrier, GROUPS - 1 + 3)
+    pl.semaphore_wait(barrier, GROUPS - 1 + 4)
 
     own = DISTANCE.index(0) * NY
     pltpu.make_async_copy(outgoing.at[own], landed.at[own], landed_sem.at[own // NY]).start()
@@ -130,13 +131,14 @@
             RIGHT2: (left_x, 0, HALF, right),
             LEFT2: (right_x, HALF, HALF, left),
             SIBLING: (pl.ds(0, NX), 0, CROWS, sibling),
+            OVER: (x, 0, CROWS, far),
         }[kind]
         piece = buffer.at[core, slots, pl.ds(start + begin, count)]
         return pltpu.make_async_remote_copy(
             src_ref=piece,
             dst_ref=piece,
             send_sem=send.at[kind],
-            recv_sem=recv.at[FAR if kind == LEFT2 else kind, chunk],
+            recv_sem=recv.at[FAR if kind in (LEFT2, OVER) else kind, chunk],
             device_id=(me_g, target),
             device_id_type=MESH,
         )
@@ -168,6 +170,11 @@
 
     def third(kit, chunk):
         arrival(kit[0], kit[2], FAR, chunk)
+        ring(*kit, SIBLING, chunk).start()
+
+    def all_over(kit, chunk):
+        for kind in (RIGHT, LEFT, FAR):
+            arrival(kit[0], kit[2], kind, chunk)
         ring(*kit, SIBLING, chunk).start()
 
     def gathered(kit, chunk):
@@ -233,31 +240,13 @@
         def _():
             third(x_ring, i - 1)
 
-        @pl.when(i >= 3)
-        def _():
-            third(h_ring, i - 3)
-
         @pl.when(i < CHUNKS)
         def _():
             second(x_ring, i)
 
-        @pl.when(i + AHEAD < CHUNKS)
-        def _():
-            begin_rows(i + AHEAD)
-
-        @pl.when(i == 3)
-        def _():
-            weights[2].wait()
-
-        @pl.when(i >= 3)
-        def _():
-            gathered(h_ring, i - 3)
-            output_rows(i - 3)
-            send_back(i - 3)
-
-        @pl.when((i >= 2) & (i < CHUNKS + 2))
-        def _():
-            second(h_ring, i - 2)
+        @pl.when(i >= 2)
+        def _():
+            all_over(h_ring, i - 2)
 
         @pl.when(i == 1)
         def _():
@@ -268,12 +257,26 @@
         def _():
             gathered(x_ring, i - 1)
             hidden_rows(i - 1)
-            for kind in (RIGHT, LEFT):
+            for kind in (RIGHT, LEFT, OVER):
                 ring(*h_ring, kind, i - 1).start()
 
+        @pl.when(i + AHEAD < CHUNKS)
+        def _():
+            begin_rows(i + AHEAD)
+
+        @pl.when(i == 2)
+        def _():
+            weights[2].wait()
+
+        @pl.when(i >= 2)
+        def _():
+            gathered(h_ring, i - 2)
+            output_rows(i - 2)
+            send_back(i - 2)
+
         return carry
 
-    lax.fori_loop(0, CHUNKS + 3, turn, 0)
+    lax.fori_loop(0, CHUNKS + 2, turn, 0)
 
     def collect(chunk, carry):
         combine(chunk)
@@ -282,15 +285,19 @@
     lax.fori_loop(0, CHUNKS, collect, 0)
     out_ref[...] = total[...].astype(BF16)
 
-    for buffer, send, _ in (x_ring, h_ring):
-        for kind, piece in (
-            (RIGHT, buffer.at[core, x]),
-            (LEFT, buffer.at[core, x]),
-            (RIGHT2, buffer.at[core, left_x, pl.ds(0, ROWS // 2)]),
-            (LEFT2, buffer.at[core, right_x, pl.ds(0, ROWS // 2)]),
-            (SIBLING, buffer.at[core]),
-        ):
-            pltpu.make_async_copy(piece, piece, send.at[kind]).wait()
+    half = pl.ds(0, ROWS // 2)
+    for send, kind, piece in (
+        (x_send, RIGHT, rows.at[core, x]),
+        (x_send, LEFT, rows.at[core, x]),
+        (x_send, RIGHT2, rows.at[core, left_x, half]),
+        (x_send, LEFT2, rows.at[core, right_x, half]),
+        (x_send, SIBLING, rows.at[core]),
+        (h_send, RIGHT, hidden.at[core, x]),
+        (h_send, LEFT, hidden.at[core, x]),
+        (h_send, OVER, hidden.at[core, x]),
+        (h_send, SIBLING, hidden.at[core]),
+    ):
+        pltpu.make_async_copy(piece, piece, send.at[kind]).wait()
     others = pl.ds(0, GROUPS - 1)
     pltpu.make_async_copy(outgoing.at[others], outgoing.at[others], sent_sem.at[0]).wait()
     pltpu.make_async_copy(results.at[others], results.at[others], back_sem.at[0]).wait()
@@ -321,10 +328,10 @@
             dma((CHUNKS,)),
             dma((1,)),
             dma((CHUNKS,)),
-            dma((5,)),
-            dma((5, CHUNKS)),
-            dma((5,)),
-            dma((5, CHUNKS)),
+            dma((6,)),
+            dma((6, CHUNKS)),
+            dma((6,)),
+            dma((6, CHUNKS)),
         ],
         compiler_params=pltpu.CompilerParams(
             collective_id=0, has_side_effects=True, vmem_limit_bytes=56 * 1024 * 1024

time: 105 us -> 101 us (0.962); the launches traced: 103 us -> 101 us
  Pallas kernels: 103 us -> 100 us
    pallas_call x1, Pallas kernels: 103 us -> 100 us  [on_device(): pl.pallas_call(kernel, out_shape=pltpu.VMEM((TOK, FEAT), BF16), in_specs=...]
where the time goes in v4:
time: 101 us
  Pallas kernels  100 us (99%)
    pallas_call x1, Pallas kernels, on_device(): pl.pallas_call(kernel, out_shape=pltpu.VMEM((TOK, FEAT), BF16), in_specs=...  100 us

profile of v4, /device:TPU:97, one launch (start us, length us, event | category | flops | bytes accessed | tf_op | source)
XLA Modules:
  0.0 100.7 jit_solution(12435467663267117987)
XLA Ops:
  0.0 100.1 %shard_map.64 = bf16[64,896]{1,0:T(8,128)(2,1)S(1)} custom-call(bf16[64,896]{1,0:T(8,128)(2,1)} %tokens_ref.1, s32[8,64]{1,0:T(8,128)} %bitcast.2, f32[8,64]{1,0:T(8,128)} %bitcast.3, bf16[1,7168,256]{2,1,0:T(8,128)(2,1)} %gate_hbm.1, bf16[1,7168,256]{2,1,0:T(8,128)(2,1)} %up_hbm.1, bf16[1,2048,896]{2,1,0:T(8,128)(2,1)} %down_hbm.1), custom_call_target="tpu_custom_call" | custom-call | flops 8499999744 | bytes 11500000 | tf_op jit(solution)/shard_map/pallas_call | solution.py:309
  100.1 0.6 copy.8

commit v5 on v4

--- a/solution.py
+++ b/solution.py
@@ -260,10 +260,6 @@
             for kind in (RIGHT, LEFT, OVER):
                 ring(*h_ring, kind, i - 1).start()
 
-        @pl.when(i + AHEAD < CHUNKS)
-        def _():
-            begin_rows(i + AHEAD)
-
         @pl.when(i == 2)
         def _():
             weights[2].wait()
@@ -273,6 +269,10 @@
             gathered(h_ring, i - 2)
             output_rows(i - 2)
             send_back(i - 2)
+
+        @pl.when(i + AHEAD < CHUNKS)
+        def _():
+            begin_rows(i + AHEAD)
 
         return carry
 

time: 101 us -> 101 us (level)
  no operation moved by 1% of the time
where the time goes in v5:
time: 101 us
  Pallas kernels  100 us (99%)
    pallas_call x1, Pallas kernels, on_device(): pl.pallas_call(kernel, out_shape=pltpu.VMEM((TOK, FEAT), BF16), in_specs=...  100 us

profile of v5, /device:TPU:97, one launch (start us, length us, event | category | flops | bytes accessed | tf_op | source)
XLA Modules:
  0.0 100.7 jit_solution(12520074475418320230)
XLA Ops:
  0.0 100.1 %shard_map.64 = bf16[64,896]{1,0:T(8,128)(2,1)S(1)} custom-call(bf16[64,896]{1,0:T(8,128)(2,1)} %tokens_ref.1, s32[8,64]{1,0:T(8,128)} %bitcast.2, f32[8,64]{1,0:T(8,128)} %bitcast.3, bf16[1,7168,256]{2,1,0:T(8,128)(2,1)} %gate_hbm.1, bf16[1,7168,256]{2,1,0:T(8,128)(2,1)} %up_hbm.1, bf16[1,2048,896]{2,1,0:T(8,128)(2,1)} %down_hbm.1), custom_call_target="tpu_custom_call" | custom-call | flops 8499999744 | bytes 11500000 | tf_op jit(solution)/shard_map/pallas_call | solution.py:309
  100.1 0.6 copy.8
